TPU v7x, 32 devices: a whole 2x2x4 slice. The times are simulated.
32 devices in a mesh: comp: 2 (over x), lat: 4 (over y, core), lon: 4 (over z).
Axes of the slice: x: 2, y: 2, z: 4, core: 2. Of those that a mesh axis runs over, the one named last changes fastest.
Arguments:
- state: bfloat16 [2, 80, 8, 1024], P('comp', None, 'lat', 'lon'), may hold values from -6 to 6
- direction: bfloat16 [2, 80, 8, 1024], P('comp', None, 'lat', 'lon'), may hold values from -6 to 6
- air_first: bfloat16 [9, 512, 80], replicated, may hold values from -0.21875 to 0.21875
- air_bias: float32 [512], replicated, may hold values from -4 to 4
- air_second: bfloat16 [9, 80, 512], replicated, may hold values from -0.09375 to 0.09375
- air_flux: bfloat16 [2, 80], replicated, may hold values from -1.25 to 1.25
- aloft_reaction_to_seawarmth: float32 [80], replicated, may hold values from -4 to 4
- sea_first: bfloat16 [9, 256, 40], replicated, may hold values from -0.3125 to 0.3125
- sea_bias: float32 [256], replicated, may hold values from -4 to 4
- sea_second: bfloat16 [9, 40, 256], replicated, may hold values from -0.125 to 0.125
- sea_forcing: bfloat16 [40, 2], replicated, may hold values from -4 to 4
- regrid_index: int32 [2, 8, 8, 1024], P('comp', None, 'lat', 'lon'), may hold values from 0 to 2047, as said below
- regrid_weight: int32 [2, 8, 8, 1024], P('comp', None, 'lat', 'lon'), may hold values from 1 to 255
- land_mask: int32 [2, 8, 1024], P(None, 'lat', 'lon'), may hold values 0 or 1
Outputs:
- image: bfloat16 [2, 80, 8, 1024], P('comp', None, 'lat', 'lon')
- product: bfloat16 [2, 80, 8, 1024], P('comp', None, 'lat', 'lon')
Inputs may be any that keep to these rules, and one draw needn't show every extreme that they name: `regrid_index`: in block 0, entries number cells of the fine window of the tile that holds the cell (below 2048); in block 1 they number cells of its coarse window (below 1024); the sources of a cell lie near it.
All inputs are finite; a program needn't handle non-finite values. No bound on the sum of `land_mask` on one device may be relied on, other than what follows from the above.
Results may differ from a plain program's by a relative error of at most 0.0064.
Values may be sent and summed in bfloat16 or wider, within the bound.
A program may use at most 64 MiB of HBM per device.

v0:
```python
import functools

import jax
import jax.numpy as jnp
from jax import lax
from jax.experimental import pallas as pl
from jax.experimental.pallas import tpu as pltpu
from jax.sharding import PartitionSpec as P

MESH = pl.DeviceIdType.MESH
F32 = jnp.float32
BF16 = jnp.bfloat16
LANES = 128
TILE_WAYS = ((-1, 0), (1, 0))
EDGE_WAYS = ((0, -1), (0, 1), (-1, -1), (-1, 1), (1, -1), (1, 1))
WAYS = TILE_WAYS + EDGE_WAYS


def dot(a, b):
    return jnp.dot(a, b, preferred_element_type=F32)


def split_dot(a, b, dims):
    high = a.astype(BF16)
    low = (a - high.astype(F32)).astype(BF16)
    both = lax.dot_general(
        jnp.concatenate([high, low], axis=0), b, (dims, ((), ())), preferred_element_type=F32
    )
    return both[: a.shape[0]] + both[a.shape[0] :]


def pack_edges(tile, rows, columns):
    lane = lax.broadcasted_iota(jnp.int32, (tile.shape[0], LANES), 1)
    packed = None
    for r in range(rows):
        first = tile[:, r * columns : r * columns + LANES]
        last = tile[:, (r + 1) * columns - LANES : (r + 1) * columns]
        part = jnp.where(lane < 2, first, jnp.where(lane >= LANES - 2, last, 0.0))
        if r:
            part = pltpu.roll(part, LANES // rows * r, 1)
        packed = part if packed is None else packed + part
    return packed


def wide_row(main, left, right, r, rows):
    lane = lax.broadcasted_iota(jnp.int32, left.shape, 1)
    if r:
        back = LANES - LANES // rows * r
        left, right = pltpu.roll(left, back, 1), pltpu.roll(right, back, 1)
    side = jnp.where(lane < 2, right, jnp.where(lane >= LANES - 2, left, 0.0))
    return jnp.concatenate([main, side], axis=1)


def three(row, forward):
    width = row.shape[1]
    before, after = pltpu.roll(row, 1, 1), pltpu.roll(row, width - 1, 1)
    parts = [before, row, after] if forward else [after, row, before]
    return jnp.concatenate(parts, axis=0)


def fold_three(stack, forward, columns):
    k = stack.shape[0] // 3
    width = stack.shape[1]
    first, mid, last = stack[:k], stack[k : 2 * k], stack[2 * k :]
    one, other = (1, width - 1) if forward else (width - 1, 1)
    return (pltpu.roll(first, one, 1) + mid + pltpu.roll(last, other, 1))[:, :columns]


def kernel(
    cfg,
    state_hbm, direction_hbm, index_hbm, weight_hbm, mask_hbm,
    air_bias_hbm, air_flux_hbm, react_hbm, sea_bias_hbm, sea_force_hbm,
    aw1_hbm, aw2_hbm, sw1_hbm, sw2_hbm,
    image_ref,
    product_ref,
    raw, wide_raw, index_raw, weight_raw, mask_raw,
    air_bias, air_flux, react_in, sea_bias, sea_force, slim,
    aw1_raw, aw2_raw, sw1_raw, sw2_raw, load,
    aw1, aw1t, aw2, aw2t,
    sw1, sw1t, sw2, sw2t,
    inp,
    edge_a, tiles_a, edges_a,
    cot, edge_b, tiles_b, edges_b,
    pay, paid, out_win, in_win,
    onehot, share_hi, values,
    ax, av, aslope, az,
    sx, sv, sslope, sz,
    send_a, recv_a, send_b, recv_b, send_c, recv_c, send_d, recv_d,
):
    rows, columns, lat_n, lon_n, air_k, air_h, sea_k, sea_h = cfg
    cells = rows * columns
    comp, lat, lon = (lax.axis_index(a) for a in ("comp", "lat", "lon"))
    is_air = comp == 0
    is_sea = comp == 1
    mine = {"comp": comp, "lat": lat, "lon": lon}
    del mine

    def exists(dl):
        return lat + dl >= 0 if dl < 0 else lat + dl < lat_n

    def there(dl, dn):
        return (comp, (lat + dl + lat_n) % lat_n, (lon + dn + lon_n) % lon_n)

    def across(dn):
        return (1 - comp, lat, (lon + dn + lon_n) % lon_n)

    def when(dl, act):
        if dl == 0:
            act()
        else:
            pl.when(exists(dl))(act)

    fetch = [pltpu.make_async_copy(src, dst, load.at[i]) for i, (src, dst) in enumerate((
        (state_hbm, raw.at[0]), (direction_hbm, raw.at[1]),
        (index_hbm, index_raw), (weight_hbm, weight_raw), (mask_hbm, mask_raw),
        (air_bias_hbm, air_bias), (air_flux_hbm, air_flux), (react_hbm, react_in),
        (sea_bias_hbm, sea_bias), (sea_force_hbm, sea_force),
        (aw1_hbm, aw1_raw), (aw2_hbm, aw2_raw), (sw1_hbm, sw1_raw), (sw2_hbm, sw2_raw)))]
    for c in fetch[:10]:
        c.start()

    @pl.when(is_air)
    def _():
        for c in fetch[10:12]:
            c.start()

    @pl.when(is_sea)
    def _():
        for c in fetch[12:14]:
            c.start()

    barrier = pltpu.get_barrier_semaphore()
    for dl, dn in WAYS:
        when(dl, lambda dl=dl, dn=dn: pl.semaphore_signal(
            barrier, inc=1, device_id=there(dl, dn), device_id_type=MESH))
    for dn in (-1, 0, 1):
        pl.semaphore_signal(barrier, inc=1, device_id=across(dn), device_id_type=MESH)

    def halo(tile, edge, tiles, edges, send, recv):
        copies = []
        for i, (dl, dn) in enumerate(WAYS):
            n = i - len(TILE_WAYS)
            copies.append(pltpu.make_async_remote_copy(
                src_ref=tile if n < 0 else edge,
                dst_ref=tiles.at[i] if n < 0 else edges.at[n],
                send_sem=send.at[i], recv_sem=recv.at[i],
                device_id=there(dl, dn), device_id_type=MESH))
        return copies

    def clear(tiles, edges):
        for i, (dl, dn) in enumerate(WAYS):
            n = i - len(TILE_WAYS)

            def act(i=i, n=n):
                if n < 0:
                    tiles[i] = jnp.zeros(tiles.shape[1:], BF16)
                else:
                    edges[n] = jnp.zeros(edges.shape[1:], BF16)

            if dl:
                pl.when(jnp.logical_not(exists(-dl)))(act)

    def start(copies):
        for (dl, dn), c in zip(WAYS, copies):
            when(dl, c.start)

    def wait_recv(copies):
        for (dl, dn), c in zip(WAYS, copies):
            when(-dl, c.wait_recv)

    def wait_send(copies):
        for (dl, dn), c in zip(WAYS, copies):
            when(dl, c.wait_send)

    halo_a = halo(inp, edge_a, tiles_a, edges_a, send_a, recv_a)
    halo_b = halo(cot, edge_b, tiles_b, edges_b, send_b, recv_b)
    pays = [pltpu.make_async_remote_copy(
        src_ref=pay, dst_ref=paid.at[i], send_sem=send_c.at[i], recv_sem=recv_c.at[i],
        device_id=across(dn), device_id_type=MESH) for i, dn in enumerate((0, -1))]
    wins = [pltpu.make_async_remote_copy(
        src_ref=out_win, dst_ref=in_win.at[i], send_sem=send_d.at[i], recv_sem=recv_d.at[i],
        device_id=across(dn), device_id_type=MESH) for i, dn in enumerate((0, 1))]

    for i in range(2):
        fetch[i].wait()
        wide_raw[...] = raw[i].astype(F32)
        channels = raw.shape[1]
        for r in range(rows):
            inp[i * channels : (i + 1) * channels, r * columns : (r + 1) * columns] = (
                wide_raw[:, r, :].astype(BF16))
    edge_a[...] = pack_edges(inp[...].astype(F32), rows, columns).astype(BF16)
    pay[...] = jnp.zeros(pay.shape, F32)

    @pl.when(is_sea)
    def _():
        base = 2 * sea_k
        centre = inp[base : 2 * base, :].astype(F32)
        pay[0:1, :] = centre[0:1]
        pay[1:2, :] = centre[sea_k : sea_k + 1]

    up = jnp.where(exists(-1), 3, 0)
    down = jnp.where(exists(1), 3, 0)
    pl.semaphore_wait(barrier, 5 + up + down)
    start(halo_a)

    @pl.when(is_sea)
    def _():
        for c in pays:
            c.start()

    clear(tiles_a, edges_a)
    clear(tiles_b, edges_b)

    for c in fetch[2:10]:
        c.wait()
    index = jnp.concatenate([index_raw[:, r, :] for r in range(rows)], axis=1)
    weight = jnp.concatenate([weight_raw[:, r, :] for r in range(rows)], axis=1).astype(F32)
    slim[...] = jnp.zeros(slim.shape, F32)
    slim[0:1, 0:air_h] = air_bias[...]
    slim[1:2, 0:sea_h] = sea_bias[...]
    slim[2:4, 0:air_k] = air_flux[...].astype(F32)
    slim[4:5, 0:air_k] = react_in[...]
    slim[5:7, 0:sea_k] = sea_force[...].astype(F32)
    par = jnp.transpose(slim[...])
    share_bias = par[0:air_h, 0:1], par[0:sea_h, 1:2]

    def lay_out(first_raw, second_raw, w1, w1t, w2, w2t):
        hidden, deep = first_raw.shape[2], w1.shape[1] // 3
        blank = jnp.zeros((deep - first_raw.shape[1], hidden), F32)
        for a in range(3):
            back = 2 - a
            tall = lambda ref: jnp.concatenate([ref[a].astype(F32), blank], axis=0)
            w1[:, a * deep : (a + 1) * deep] = jnp.transpose(tall(first_raw)).astype(BF16)
            w2t[:, back * deep : (back + 1) * deep] = jnp.transpose(tall(second_raw)).astype(BF16)
            w1t[:, back * hidden : (back + 1) * hidden] = first_raw[a]
            w2[:, a * hidden : (a + 1) * hidden] = second_raw[a]

    @pl.when(is_air)
    def _():
        for c in fetch[10:12]:
            c.wait()
        lay_out(aw1_raw, aw2_raw, aw1, aw1t, aw2, aw2t)

    @pl.when(is_sea)
    def _():
        for c in fetch[12:14]:
            c.wait()
        lay_out(sw1_raw, sw2_raw, sw1, sw1t, sw2, sw2t)

    near = jnp.sum(weight[0:4], axis=0, keepdims=True)
    far = jnp.sum(weight[4:8], axis=0, keepdims=True)
    slot8 = lax.broadcasted_iota(jnp.int32, weight.shape, 0)
    total = jnp.where(is_air, near + far, jnp.where(slot8 < 4, near, far))
    share = weight / total
    high = lax.shift_right_logical(index, LANES.bit_length() - 1)
    low = index & (LANES - 1)
    place = lax.broadcasted_iota(jnp.int32, (LANES, cells), 0)
    wrows = values.shape[0]
    row16 = lax.broadcasted_iota(jnp.int32, (wrows, cells), 0)
    row16 = jnp.where(is_air, row16, row16 % (wrows // 2))
    for s in range(8):
        onehot[:, s * cells : (s + 1) * cells] = jnp.where(
            place == low[s : s + 1], 1.0, 0.0).astype(BF16)
        share_hi[:, s * cells : (s + 1) * cells] = jnp.where(
            row16 == high[s : s + 1], share[s : s + 1], 0.0)

    per = columns // LANES

    def gather():
        for f in range(2):
            for r in range(rows):
                for nxt in range(2):
                    for h in range(per):
                        at = ((f * rows + r) * 2 + nxt) * per + h
                        lane0 = r * columns + h * LANES
                        values[at : at + 1, :] = paid[nxt, f : f + 1, lane0 : lane0 + LANES]
        got = split_dot(values[...], onehot[...], ((1,), (0,))) * share_hi[...]
        parts = [got[:, s * cells : (s + 1) * cells] for s in range(8)]
        return sum(parts[1:4], parts[0]), sum(parts[5:8], parts[4])

    def scatter(first, second):
        spread = jnp.concatenate([first] * 4 + [second] * 4, axis=1) * share_hi[...]
        out_win[...] = split_dot(spread, onehot[...], ((1,), (1,)))

    def arrived():
        fields = []
        for f in range(2):
            pieces = []
            for r in range(rows):
                for h in range(per):
                    own = ((f * rows + r) * 2) * per + h
                    pieces.append(in_win[0, own : own + 1, :] + in_win[1, own + per : own + per + 1, :])
            fields.append(jnp.concatenate(pieces, axis=1))
        return fields

    def place_of(q, split):
        height = rows * split
        where = -1 if q < 0 else (1 if q >= height else 0)
        q = q - where * height
        return where, q // rows, q % rows

    def stacks(tile, tiles, edges, base, k, split, forward, dst):
        lo, hi = base, base + k * split
        own = tile[lo:hi, :].astype(F32)
        above, below = tiles[1, lo:hi, :].astype(F32), tiles[0, lo:hi, :].astype(F32)
        edge = [edges[n, lo:hi, :].astype(F32) for n in range(6)]
        lefts = {0: edge[1], -1: edge[5], 1: edge[3]}
        rights = {0: edge[0], -1: edge[4], 1: edge[2]}
        mains = {0: own, -1: above, 1: below}
        for p in range(rows * split + 4):
            where, s, r = place_of(p - 2, split)
            ch = slice(s * k, (s + 1) * k)
            row = wide_row(mains[where][ch, r * columns : (r + 1) * columns],
                           lefts[where][ch], rights[where][ch], r, rows)
            dst[p] = jnp.concatenate(
                [three(row, forward), jnp.zeros((dst.shape[1] - 3 * k, row.shape[1]), F32)],
                axis=0).astype(BF16)

    def keep(p, height):
        gone = ((p == 0) & (lat == 0)) | ((p == height + 1) & (lat == lat_n - 1))
        return jnp.where(gone, 0.0, 1.0)

    def rows_of(ref, p):
        return ref[pl.ds(p, 3)].reshape(3 * ref.shape[1], ref.shape[2])

    def give(out, value):
        for r in range(rows):
            wide_raw[:, r, :] = value[:, r * columns : (r + 1) * columns]
        out[...] = wide_raw[...].astype(BF16)

    def first_conv(w1, bias, x, v, slope, z, height):
        def body(p, carry):
            pre = dot(w1[...], rows_of(x, p)) + bias
            t = jnp.tanh(pre)
            s = 1.0 - t * t
            slope[p] = s
            lin = dot(w1[...], rows_of(v, p))
            z[p] = (s * keep(p, height) * lin).astype(BF16)
            return carry
        lax.fori_loop(0, height + 2, body, 0)

    def second_conv(w2, z, height):
        return [fold_three(dot(w2[...], rows_of(z, i)), True, columns) for i in range(height)]

    def second_back(w2t, c, slope, z, height):
        def body(p, carry):
            lin = dot(w2t[...], rows_of(c, p))
            z[p] = (slope[p] * keep(p, height) * lin).astype(BF16)
            return carry
        lax.fori_loop(0, height + 2, body, 0)

    def first_back(w1t, z, height):
        return [fold_three(dot(w1t[...], rows_of(z, i)), False, columns) for i in range(height)]

    def packed(fine, split):
        parts = [jnp.concatenate(fine[s * rows : (s + 1) * rows], axis=1) for s in range(split)]
        return parts

    flux0, flux1 = par[0:air_k, 2:3], par[0:air_k, 3:4]
    react = par[0:air_k, 4:5]
    force0, force1 = par[0:sea_k, 5:6], par[0:sea_k, 6:7]
    half_rows = wrows // 2
    wait_recv(halo_a)

    @pl.when(is_air)
    def _():
        stacks(inp, tiles_a, edges_a, 0, air_k, 1, True, ax)
        stacks(inp, tiles_a, edges_a, air_k, air_k, 1, True, av)
        first_conv(aw1, share_bias[0], ax, av, aslope, az, rows)
        y = packed(second_conv(aw2, az, rows), 1)[0]
        pay[0:1, :] = jnp.sum(flux0 * y, axis=0, keepdims=True)
        pay[1:2, :] = jnp.sum(flux1 * y, axis=0, keepdims=True)
        for c in pays:
            c.start()
        for c in pays:
            c.wait_recv()
        near, far = gather()
        lifted = jnp.sum(near + far, axis=0, keepdims=True)
        image = (y + react * lifted).astype(BF16)
        wide = image.astype(F32)
        give(image_ref, wide)
        surface = jnp.sum(react * wide, axis=0, keepdims=True)
        source = jnp.broadcast_to(surface, (wrows, cells))
        scatter(source, source)
        for c in wins:
            c.start()
        for c in wins:
            c.wait_recv()
        back0, back1 = arrived()
        total = wide + (flux0 * back0 + flux1 * back1)
        cot[...] = total.astype(BF16)
        edge_b[...] = pack_edges(cot[...].astype(F32), rows, columns).astype(BF16)

    @pl.when(is_sea)
    def _():
        stacks(inp, tiles_a, edges_a, 0, sea_k, 2, True, sx)
        stacks(inp, tiles_a, edges_a, 2 * sea_k, sea_k, 2, True, sv)
        first_conv(sw1, share_bias[1], sx, sv, sslope, sz, 2 * rows)
        ys = packed(second_conv(sw2, sz, 2 * rows), 2)
        for c in pays:
            c.wait_recv()
        images, sources = [], []
        row_at = lax.broadcasted_iota(jnp.int32, (wrows, cells), 0)
        for t, got in enumerate(gather()):
            f0 = jnp.sum(got[:half_rows], axis=0, keepdims=True)
            f1 = jnp.sum(got[half_rows:], axis=0, keepdims=True)
            mask = jnp.concatenate(
                [mask_raw[t, r : r + 1, :] for r in range(rows)], axis=1).astype(F32)
            one = (mask * (ys[t] + (force0 * f0 + force1 * f1))).astype(BF16).astype(F32)
            images.append(one)
            pulled0 = jnp.sum(force0 * one, axis=0, keepdims=True)
            pulled1 = jnp.sum(force1 * one, axis=0, keepdims=True)
            sources.append(jnp.where(row_at < half_rows, pulled0, pulled1))
        scatter(*sources)
        for c in wins:
            c.start()
        image = jnp.concatenate(images, axis=0).astype(BF16)
        cot[...] = image
        edge_b[...] = pack_edges(image.astype(F32), rows, columns).astype(BF16)

    start(halo_b)

    @pl.when(is_sea)
    def _():
        give(image_ref, cot[...].astype(F32))

    wait_recv(halo_b)

    @pl.when(is_air)
    def _():
        stacks(cot, tiles_b, edges_b, 0, air_k, 1, False, ax)
        second_back(aw2t, ax, aslope, az, rows)
        give(product_ref, packed(first_back(aw1t, az, rows), 1)[0])

    @pl.when(is_sea)
    def _():
        stacks(cot, tiles_b, edges_b, 0, sea_k, 2, False, sx)
        second_back(sw2t, sx, sslope, sz, 2 * rows)
        fine = packed(first_back(sw1t, sz, 2 * rows), 2)
        for c in wins:
            c.wait_recv()
        top = lax.broadcasted_iota(jnp.int32, (sea_k, cells), 0) == 0
        fine = [f + jnp.where(top, b, 0.0) for f, b in zip(fine, arrived())]
        give(product_ref, jnp.concatenate(fine, axis=0))

    for c in pays + wins:
        c.wait_send()
    wait_send(halo_a)
    wait_send(halo_b)


def shards(
    lat_n, lon_n, state, direction, air_first, air_bias, air_second, air_flux, reaction,
    sea_first, sea_bias, sea_second, sea_forcing, regrid_index, regrid_weight, land_mask,
):
    channels, rows, columns = state.shape[1:]
    cells = rows * columns
    air_h, air_k = air_first.shape[1:]
    sea_h, sea_k = sea_first.shape[1:]
    def rowed(w):
        return w.reshape(3, 3 * w.shape[1], w.shape[2])

    args = [
        state[0], direction[0], regrid_index[0], regrid_weight[0], land_mask,
        air_bias[None], air_flux, reaction[None], sea_bias[None], sea_forcing.T,
        rowed(air_first.transpose(0, 2, 1)), rowed(air_second),
        rowed(sea_first.transpose(0, 2, 1)), rowed(sea_second),
    ]
    air_deep, sea_deep = 3 * air_k + -3 * air_k % LANES, 3 * sea_k + -3 * sea_k % LANES
    tall = max(air_h, sea_h)
    wide = columns + LANES
    wrows = 2 * rows * 2 * columns // LANES
    dma = pltpu.SemaphoreType.DMA
    vmem = pltpu.VMEM
    image, product = pl.pallas_call(
        functools.partial(kernel, (rows, columns, lat_n, lon_n, air_k, air_h, sea_k, sea_h)),
        out_shape=[jax.ShapeDtypeStruct((channels, rows, columns), BF16)] * 2,
        in_specs=[pl.BlockSpec(memory_space=pl.ANY)] * len(args),
        out_specs=[pl.BlockSpec(memory_space=pltpu.VMEM)] * 2,
        scratch_shapes=[
            vmem((2, channels, rows, columns), BF16),
            vmem((channels, rows, columns), F32),
            vmem(args[2].shape, jnp.int32),
            vmem(args[3].shape, jnp.int32),
            vmem(args[4].shape, jnp.int32),
            *[vmem(a.shape, a.dtype) for a in args[5:10]],
            vmem((LANES, tall), F32),
            *[vmem(a.shape, a.dtype) for a in args[10:14]],
            dma((14,)),
            vmem((air_h, 3 * air_deep), BF16),
            vmem((3 * air_k, 3 * air_h), BF16),
            vmem((3 * air_k, 3 * air_h), BF16),
            vmem((air_h, 3 * air_deep), BF16),
            vmem((sea_h, 3 * sea_deep), BF16),
            vmem((3 * sea_k, 3 * sea_h), BF16),
            vmem((3 * sea_k, 3 * sea_h), BF16),
            vmem((sea_h, 3 * sea_deep), BF16),
            vmem((2 * channels, cells), BF16),
            vmem((2 * channels, LANES), BF16),
            vmem((2, 2 * channels, cells), BF16),
            vmem((6, 2 * channels, LANES), BF16),
            vmem((channels, cells), BF16),
            vmem((channels, LANES), BF16),
            vmem((2, channels, cells), BF16),
            vmem((6, channels, LANES), BF16),
            vmem((8, cells), F32),
            vmem((2, 8, cells), F32),
            vmem((wrows, LANES), F32),
            vmem((2, wrows, LANES), F32),
            vmem((LANES, 8 * cells), BF16),
            vmem((wrows, 8 * cells), F32),
            vmem((wrows, LANES), F32),
            vmem((rows + 4, air_deep, wide), BF16),
            vmem((rows + 4, air_deep, wide), BF16),
            vmem((rows + 2, air_h, wide), F32),
            vmem((rows + 2, air_h, wide), BF16),
            vmem((2 * rows + 4, sea_deep, wide), BF16),
            vmem((2 * rows + 4, sea_deep, wide), BF16),
            vmem((2 * rows + 2, sea_h, wide), F32),
            vmem((2 * rows + 2, sea_h, wide), BF16),
            dma((8,)), dma((8,)), dma((8,)), dma((8,)), dma((2,)), dma((2,)), dma((2,)), dma((2,)),
        ],
        compiler_params=pltpu.CompilerParams(
            collective_id=0, has_side_effects=True, vmem_limit_bytes=48 * 1024 * 1024),
        name="coupled",
    )(*args)
    return image[None], product[None]


def solution(mesh):
    field = P("comp", None, "lat", "lon")
    return jax.shard_map(
        functools.partial(shards, mesh.shape["lat"], mesh.shape["lon"]),
        mesh=mesh,
        in_specs=(field, field) + (P(),) * 9 + (field, field, P(None, "lat", "lon")),
        out_specs=(field, field),
        check_vma=False,
    )
```

profile of v0, /device:TPU:1, one launch (start us, length us, event | category | flops | bytes accessed | tf_op | source)
XLA Modules:
  0.0 47.3 jit_solution(9031875709145703089)
XLA Ops:
  0.6 0.0 copy-start.6
  0.6 0.0 copy-start.8
  0.7 0.0 copy-start.9
  0.7 0.0 copy-start.11
  0.7 0.7 %copy-done.6 = s32[1,8,2,256]{3,2,1,0:T(2,128)S(1)} copy-done((s32[1,8,2,256]{3,2,1,0:T(2,128)S(1)}, s32[1,8,2,256]{3,2,1,0:T(2,128)}, u32[]{:S(2)}) %copy-start.6) | copy-done | bytes 16408
  1.4 0.0 copy-done.8
  1.4 0.0 copy-done.9
  1.4 0.0 copy-done.11
  1.4 0.0 copy-start
  1.4 1.1 %copy-done = bf16[9,512,80]{1,2,0:T(8,128)(2,1)S(1)} copy-done((bf16[9,512,80]{1,2,0:T(8,128)(2,1)S(1)}, bf16[9,512,80]{1,2,0:T(8,128)(2,1)}, u32[]{:S(2)}) %copy-start) | copy-done | bytes 737304
  2.5 0.0 copy-start.1
  2.5 1.1 %copy-done.1 = bf16[9,80,512]{2,1,0:T(8,128)(2,1)S(1)} copy-done((bf16[9,80,512]{2,1,0:T(8,128)(2,1)S(1)}, bf16[9,80,512]{2,1,0:T(8,128)(2,1)}, u32[]{:S(2)}) %copy-start.1) | copy-done | bytes 737304
  3.6 0.0 copy-start.2
  3.6 0.9 %copy-done.2 = bf16[9,256,40]{1,2,0:T(8,128)(2,1)S(1)} copy-done((bf16[9,256,40]{1,2,0:T(8,128)(2,1)S(1)}, bf16[9,256,40]{1,2,0:T(8,128)(2,1)}, u32[]{:S(2)}) %copy-start.2) | copy-done | bytes 184344
  4.5 0.9 %copy-done.3 = bf16[9,40,256]{2,1,0:T(8,128)(2,1)S(1)} copy-done((bf16[9,40,256]{2,1,0:T(8,128)(2,1)S(1)}, bf16[9,40,256]{2,1,0:T(8,128)(2,1)}, u32[]{:S(2)}) %copy-start.3) | copy-done | bytes 184344
  5.4 0.9 %copy-done.4 = bf16[1,80,2,256]{3,2,1,0:T(2,128)(2,1)S(1)} copy-done((bf16[1,80,2,256]{3,2,1,0:T(2,128)(2,1)S(1)}, bf16[1,80,2,256]{3,2,1,0:T(2,128)(2,1)}, u32[]{:S(2)}) %copy-start.4) | copy-done | bytes 81944
  6.3 0.9 %copy-done.5 = bf16[1,80,2,256]{3,2,1,0:T(2,128)(2,1)S(1)} copy-done((bf16[1,80,2,256]{3,2,1,0:T(2,128)(2,1)S(1)}, bf16[1,80,2,256]{3,2,1,0:T(2,128)(2,1)}, u32[]{:S(2)}) %copy-start.5) | copy-done | bytes 81944
  7.2 0.7 %copy-done.7 = s32[1,8,2,256]{3,2,1,0:T(2,128)S(1)} copy-done((s32[1,8,2,256]{3,2,1,0:T(2,128)S(1)}, s32[1,8,2,256]{3,2,1,0:T(2,128)}, u32[]{:S(2)}) %copy-start.7) | copy-done | bytes 16408
  7.9 0.7 %copy-done.10 = f32[256]{0:T(256)S(1)} copy-done((f32[256]{0:T(256)S(1)}, f32[256]{0:T(256)}, u32[]{:S(2)}) %copy-start.10) | copy-done | bytes 1048
  8.6 0.7 %copy-done.12 = f32[80]{0:T(128)S(1)} copy-done((f32[80]{0:T(128)S(1)}, f32[80]{0:T(128)}, u32[]{:S(2)}) %copy-start.12) | copy-done | bytes 344
  9.3 0.7 %copy-done.13 = bf16[40,2]{0,1:T(2,128)(2,1)S(1)} copy-done((bf16[40,2]{0,1:T(2,128)(2,1)S(1)}, bf16[40,2]{0,1:T(2,128)(2,1)}, u32[]{:S(2)}) %copy-start.13) | copy-done | bytes 184
  9.9 36.1 %coupled.1 = (bf16[80,2,256]{2,1,0:T(2,128)(2,1)S(1)}, bf16[80,2,256]{2,1,0:T(2,128)(2,1)S(1)}) custom-call(bf16[80,2,256]{2,1,0:T(2,128)(2,1)S(1)} %bitcast.22, bf16[80,2,256]{2,1,0:T(2,128)(2,1)S(1)} %bitcast.23, s32[8,2,256]{2,1,0:T(2,128)S(1)} %bitcast.26, s32[8,2,256]{2,1,0:T(2,128)S(1)} %bitcast.27, s32[2,2,256]{2,1,0:T(2,128)S(1)} %copy-done.8, ...), custom_call_target="tpu_custom_call" | custom-call | tf_op jit(solution)/shard_map/coupled/pallas_call | solution.py:475
  46.0 0.6 %copy.18 = bf16[1,80,2,256]{3,2,1,0:T(2,128)(2,1)} copy(bf16[1,80,2,256]{3,2,1,0:T(2,128)(2,1)S(1)} %bitcast.25) | data formatting | bytes 163840
  46.6 0.6 %copy.19 = bf16[1,80,2,256]{3,2,1,0:T(2,128)(2,1)} copy(bf16[1,80,2,256]{3,2,1,0:T(2,128)(2,1)S(1)} %bitcast.24) | data formatting | bytes 163840
  (7 shorter events, 0.0 us)
Async XLA Ops:
  0.6 0.7 %copy-start.6 = (s32[1,8,2,256]{3,2,1,0:T(2,128)S(1)}, s32[1,8,2,256]{3,2,1,0:T(2,128)}, u32[]{:S(2)}) copy-start(s32[1,8,2,256]{3,2,1,0:T(2,128)} %param.25) | copy-start | bytes 49156
  0.6 0.7 %copy-start.8 = (s32[2,2,256]{2,1,0:T(2,128)S(1)}, s32[2,2,256]{2,1,0:T(2,128)}, u32[]{:S(2)}) copy-start(s32[2,2,256]{2,1,0:T(2,128)} %mask_hbm.1) | copy-start | bytes 12292
  0.7 0.7 %copy-start.9 = (f32[512]{0:T(512)S(1)}, f32[512]{0:T(512)}, u32[]{:S(2)}) copy-start(f32[512]{0:T(512)} %param.17) | copy-start | bytes 6148
  0.7 0.7 %copy-start.11 = (bf16[2,80]{1,0:T(2,128)(2,1)S(1)}, bf16[2,80]{1,0:T(2,128)(2,1)}, u32[]{:S(2)}) copy-start(bf16[2,80]{1,0:T(2,128)(2,1)} %air_flux_hbm.1) | copy-start | bytes 964
  1.4 1.1 %copy-start = (bf16[9,512,80]{1,2,0:T(8,128)(2,1)S(1)}, bf16[9,512,80]{1,2,0:T(8,128)(2,1)}, u32[]{:S(2)}) copy-start(bf16[9,512,80]{1,2,0:T(8,128)(2,1)} %param.16) | copy-start | bytes 2211844
  2.5 1.1 %copy-start.1 = (bf16[9,80,512]{2,1,0:T(8,128)(2,1)S(1)}, bf16[9,80,512]{2,1,0:T(8,128)(2,1)}, u32[]{:S(2)}) copy-start(bf16[9,80,512]{2,1,0:T(8,128)(2,1)} %param.18) | copy-start | bytes 2211844
  3.6 0.9 %copy-start.2 = (bf16[9,256,40]{1,2,0:T(8,128)(2,1)S(1)}, bf16[9,256,40]{1,2,0:T(8,128)(2,1)}, u32[]{:S(2)}) copy-start(bf16[9,256,40]{1,2,0:T(8,128)(2,1)} %param.21) | copy-start | bytes 552964
  4.5 0.9 %copy-start.3 = (bf16[9,40,256]{2,1,0:T(8,128)(2,1)S(1)}, bf16[9,40,256]{2,1,0:T(8,128)(2,1)}, u32[]{:S(2)}) copy-start(bf16[9,40,256]{2,1,0:T(8,128)(2,1)} %param.23) | copy-start | bytes 552964
  5.4 0.9 %copy-start.4 = (bf16[1,80,2,256]{3,2,1,0:T(2,128)(2,1)S(1)}, bf16[1,80,2,256]{3,2,1,0:T(2,128)(2,1)}, u32[]{:S(2)}) copy-start(bf16[1,80,2,256]{3,2,1,0:T(2,128)(2,1)} %param.14) | copy-start | bytes 245764
  6.3 0.9 %copy-start.5 = (bf16[1,80,2,256]{3,2,1,0:T(2,128)(2,1)S(1)}, bf16[1,80,2,256]{3,2,1,0:T(2,128)(2,1)}, u32[]{:S(2)}) copy-start(bf16[1,80,2,256]{3,2,1,0:T(2,128)(2,1)} %param.15) | copy-start | bytes 245764
  7.2 0.7 %copy-start.7 = (s32[1,8,2,256]{3,2,1,0:T(2,128)S(1)}, s32[1,8,2,256]{3,2,1,0:T(2,128)}, u32[]{:S(2)}) copy-start(s32[1,8,2,256]{3,2,1,0:T(2,128)} %param.26) | copy-start | bytes 49156
  7.9 0.7 %copy-start.10 = (f32[256]{0:T(256)S(1)}, f32[256]{0:T(256)}, u32[]{:S(2)}) copy-start(f32[256]{0:T(256)} %param.22) | copy-start | bytes 3076
  8.6 0.7 %copy-start.12 = (f32[80]{0:T(128)S(1)}, f32[80]{0:T(128)}, u32[]{:S(2)}) copy-start(f32[80]{0:T(128)} %param.20) | copy-start | bytes 964
  9.3 0.7 %copy-start.13 = (bf16[40,2]{0,1:T(2,128)(2,1)S(1)}, bf16[40,2]{0,1:T(2,128)(2,1)}, u32[]{:S(2)}) copy-start(bf16[40,2]{0,1:T(2,128)(2,1)} %param.24) | copy-start | bytes 484
where the time goes:
time: 47.7 us; the launch traced here: 47.3 us
  Pallas kernels  36.1 us (76%)
  local copies, waits for them, and re-layouts  10.5 us (22%)
  between operations  0.69 us (1%)
    pallas_call x1, Pallas kernels, shards(): pl.pallas_call(functools.partial(kernel, (rows, columns, lat_n, lon_n, ai...  36.1 us
    unnamed x30, local copies, waits for them, and re-layouts  10.5 us

commit v1 on v0

--- a/solution.py
+++ b/solution.py
@@ -11,6 +11,7 @@
 F32 = jnp.float32
 BF16 = jnp.bfloat16
 LANES = 128
+LINES = 16
 TILE_WAYS = ((-1, 0), (1, 0))
 EDGE_WAYS = ((0, -1), (0, 1), (-1, -1), (-1, 1), (1, -1), (1, 1))
 WAYS = TILE_WAYS + EDGE_WAYS
@@ -30,24 +31,30 @@
 
 
 def pack_edges(tile, rows, columns):
-    lane = lax.broadcasted_iota(jnp.int32, (tile.shape[0], LANES), 1)
+    channels = tile.shape[0]
+    lane = lax.broadcasted_iota(jnp.int32, (channels, LANES), 1)
     packed = None
     for r in range(rows):
         first = tile[:, r * columns : r * columns + LANES]
         last = tile[:, (r + 1) * columns - LANES : (r + 1) * columns]
         part = jnp.where(lane < 2, first, jnp.where(lane >= LANES - 2, last, 0.0))
-        if r:
-            part = pltpu.roll(part, LANES // rows * r, 1)
+        part = pltpu.roll(part, 2 + 4 * r, 1)
         packed = part if packed is None else packed + part
-    return packed
-
-
-def wide_row(main, left, right, r, rows):
-    lane = lax.broadcasted_iota(jnp.int32, left.shape, 1)
-    if r:
-        back = LANES - LANES // rows * r
-        left, right = pltpu.roll(left, back, 1), pltpu.roll(right, back, 1)
-    side = jnp.where(lane < 2, right, jnp.where(lane >= LANES - 2, left, 0.0))
+    blank = jnp.zeros((-channels % LANES, LANES), F32)
+    return jnp.transpose(jnp.concatenate([packed, blank], axis=0))[:LINES].astype(BF16)
+
+
+def unpack_edges(edges):
+    lines = [edges[n].astype(F32) for n in range(len(EDGE_WAYS))]
+    blank = jnp.zeros((LANES - LINES * len(lines), lines[0].shape[1]), F32)
+    return jnp.transpose(jnp.concatenate(lines + [blank], axis=0))
+
+
+def wide_row(main, sides, left, right, r):
+    lane = lax.broadcasted_iota(jnp.int32, sides.shape, 1)
+    before = pltpu.roll(sides, (LANES - 2 - LINES * left - 4 * r) % LANES, 1)
+    after = pltpu.roll(sides, -(LINES * right + 4 * r + 2) % LANES, 1)
+    side = jnp.where(lane < 2, after, jnp.where(lane >= LANES - 2, before, 0.0))
     return jnp.concatenate([main, side], axis=1)
 
 
@@ -160,9 +167,10 @@
             if dl:
                 pl.when(jnp.logical_not(exists(-dl)))(act)
 
-    def start(copies):
-        for (dl, dn), c in zip(WAYS, copies):
-            when(dl, c.start)
+    def start(copies, ways=WAYS):
+        for way, c in zip(WAYS, copies):
+            if way in ways:
+                when(way[0], c.start)
 
     def wait_recv(copies):
         for (dl, dn), c in zip(WAYS, copies):
@@ -188,7 +196,6 @@
         for r in range(rows):
             inp[i * channels : (i + 1) * channels, r * columns : (r + 1) * columns] = (
                 wide_raw[:, r, :].astype(BF16))
-    edge_a[...] = pack_edges(inp[...].astype(F32), rows, columns).astype(BF16)
     pay[...] = jnp.zeros(pay.shape, F32)
 
     @pl.when(is_sea)
@@ -201,7 +208,9 @@
     up = jnp.where(exists(-1), 3, 0)
     down = jnp.where(exists(1), 3, 0)
     pl.semaphore_wait(barrier, 5 + up + down)
-    start(halo_a)
+    start(halo_a, TILE_WAYS)
+    edge_a[...] = pack_edges(inp[...].astype(F32), rows, columns)
+    start(halo_a, EDGE_WAYS)
 
     @pl.when(is_sea)
     def _():
@@ -303,15 +312,15 @@
         lo, hi = base, base + k * split
         own = tile[lo:hi, :].astype(F32)
         above, below = tiles[1, lo:hi, :].astype(F32), tiles[0, lo:hi, :].astype(F32)
-        edge = [edges[n, lo:hi, :].astype(F32) for n in range(6)]
-        lefts = {0: edge[1], -1: edge[5], 1: edge[3]}
-        rights = {0: edge[0], -1: edge[4], 1: edge[2]}
+        sides = unpack_edges(edges)[lo:hi]
+        lefts = {0: 1, -1: 5, 1: 3}
+        rights = {0: 0, -1: 4, 1: 2}
         mains = {0: own, -1: above, 1: below}
         for p in range(rows * split + 4):
             where, s, r = place_of(p - 2, split)
             ch = slice(s * k, (s + 1) * k)
             row = wide_row(mains[where][ch, r * columns : (r + 1) * columns],
-                           lefts[where][ch], rights[where][ch], r, rows)
+                           sides[ch], lefts[where], rights[where], r)
             dst[p] = jnp.concatenate(
                 [three(row, forward), jnp.zeros((dst.shape[1] - 3 * k, row.shape[1]), F32)],
                 axis=0).astype(BF16)
@@ -389,7 +398,7 @@
         back0, back1 = arrived()
         total = wide + (flux0 * back0 + flux1 * back1)
         cot[...] = total.astype(BF16)
-        edge_b[...] = pack_edges(cot[...].astype(F32), rows, columns).astype(BF16)
+        edge_b[...] = pack_edges(cot[...].astype(F32), rows, columns)
 
     @pl.when(is_sea)
     def _():
@@ -416,7 +425,7 @@
             c.start()
         image = jnp.concatenate(images, axis=0).astype(BF16)
         cot[...] = image
-        edge_b[...] = pack_edges(image.astype(F32), rows, columns).astype(BF16)
+        edge_b[...] = pack_edges(image.astype(F32), rows, columns)
 
     start(halo_b)
 
@@ -468,6 +477,7 @@
     ]
     air_deep, sea_deep = 3 * air_k + -3 * air_k % LANES, 3 * sea_k + -3 * sea_k % LANES
     tall = max(air_h, sea_h)
+    line_a, line_b = 2 * channels + -2 * channels % LANES, channels + -channels % LANES
     wide = columns + LANES
     wrows = 2 * rows * 2 * columns // LANES
     dma = pltpu.SemaphoreType.DMA
@@ -475,7 +485,7 @@
     image, product = pl.pallas_call(
         functools.partial(kernel, (rows, columns, lat_n, lon_n, air_k, air_h, sea_k, sea_h)),
         out_shape=[jax.ShapeDtypeStruct((channels, rows, columns), BF16)] * 2,
-        in_specs=[pl.BlockSpec(memory_space=pl.ANY)] * len(args),
+        in_specs=[pl.BlockSpec(memory_space=pltpu.HBM)] * len(args),
         out_specs=[pl.BlockSpec(memory_space=pltpu.VMEM)] * 2,
         scratch_shapes=[
             vmem((2, channels, rows, columns), BF16),
@@ -496,13 +506,13 @@
             vmem((3 * sea_k, 3 * sea_h), BF16),
             vmem((sea_h, 3 * sea_deep), BF16),
             vmem((2 * channels, cells), BF16),
-            vmem((2 * channels, LANES), BF16),
+            vmem((LINES, line_a), BF16),
             vmem((2, 2 * channels, cells), BF16),
-            vmem((6, 2 * channels, LANES), BF16),
+            vmem((6, LINES, line_a), BF16),
             vmem((channels, cells), BF16),
-            vmem((channels, LANES), BF16),
+            vmem((LINES, line_b), BF16),
             vmem((2, channels, cells), BF16),
-            vmem((6, channels, LANES), BF16),
+            vmem((6, LINES, line_b), BF16),
             vmem((8, cells), F32),
             vmem((2, 8, cells), F32),
             vmem((wrows, LANES), F32),
@@ -521,7 +531,7 @@
             dma((8,)), dma((8,)), dma((8,)), dma((8,)), dma((2,)), dma((2,)), dma((2,)), dma((2,)),
         ],
         compiler_params=pltpu.CompilerParams(
-            collective_id=0, has_side_effects=True, vmem_limit_bytes=48 * 1024 * 1024),
+            collective_id=0, has_side_effects=True, vmem_limit_bytes=62 * 1024 * 1024),
         name="coupled",
     )(*args)
     return image[None], product[None]

time: 47.7 us -> 36.6 us (0.77)
  local copies, waits for them, and re-layouts: 10.5 us -> 2.25 us
  Pallas kernels: 36.1 us -> 33.5 us
    unnamed x30 -> x4, local copies, waits for them, and re-layouts: 10.5 us -> 2.25 us
    pallas_call x1, Pallas kernels: 36.1 us -> 33.5 us  [shards(): pl.pallas_call(functools.partial(kernel, (rows, columns, lat_n, lon_n, ai...]
where the time goes in v1:
time: 36.6 us; the launch traced here: 36.4 us
  Pallas kernels  33.5 us (92%)
  local copies, waits for them, and re-layouts  2.25 us (6%)
  between operations  0.65 us (2%)
    pallas_call x1, Pallas kernels, shards(): pl.pallas_call(functools.partial(kernel, (rows, columns, lat_n, lon_n, ai...  33.5 us
    unnamed x4, local copies, waits for them, and re-layouts  2.25 us

profile of v1, /device:TPU:1, one launch (start us, length us, event | category | flops | bytes accessed | tf_op | source)
XLA Modules:
  0.0 36.4 jit_solution(13178393647392184108)
XLA Ops:
  0.6 33.5 %coupled.1 = (bf16[80,2,256]{2,1,0:T(2,128)(2,1)}, bf16[80,2,256]{2,1,0:T(2,128)(2,1)}) custom-call(bf16[80,2,256]{2,1,0:T(2,128)(2,1)} %bitcast.22, bf16[80,2,256]{2,1,0:T(2,128)(2,1)} %bitcast.23, s32[8,2,256]{2,1,0:T(2,128)} %bitcast.26, s32[8,2,256]{2,1,0:T(2,128)} %bitcast.27, s32[2,2,256]{2,1,0:T(2,128)} %mask_hbm.1, f32[1,512]{1,0:T(1,128)} %bitcast.28, ...), custom_call_target="tpu_custom_call" | custom-call | tf_op jit(solution)/shard_map/coupled/pallas_call | solution.py:485
  34.2 0.0 copy-start
  34.2 1.6 %copy.18 = bf16[1,80,2,256]{3,2,1,0:T(2,128)(2,1)} copy(bf16[1,80,2,256]{3,2,1,0:T(2,128)(2,1)} %bitcast.25) | data formatting | bytes 163840
  35.8 0.0 copy-done
  35.8 0.6 %copy.19 = bf16[1,80,2,256]{3,2,1,0:T(2,128)(2,1)} copy(bf16[1,80,2,256]{3,2,1,0:T(2,128)(2,1)S(1)} %bitcast.24) | data formatting | bytes 163840
Async XLA Ops:
  34.2 1.6 %copy-start = (bf16[80,2,256]{2,1,0:T(2,128)(2,1)S(1)}, bf16[80,2,256]{2,1,0:T(2,128)(2,1)}, u32[]{:S(2)}) copy-start(bf16[80,2,256]{2,1,0:T(2,128)(2,1)} %get-tuple-element.5) | copy-start | bytes 245764

commit v2 on v1

--- a/solution.py
+++ b/solution.py
@@ -222,8 +222,6 @@
 
     for c in fetch[2:10]:
         c.wait()
-    index = jnp.concatenate([index_raw[:, r, :] for r in range(rows)], axis=1)
-    weight = jnp.concatenate([weight_raw[:, r, :] for r in range(rows)], axis=1).astype(F32)
     slim[...] = jnp.zeros(slim.shape, F32)
     slim[0:1, 0:air_h] = air_bias[...]
     slim[1:2, 0:sea_h] = sea_bias[...]
@@ -233,46 +231,64 @@
     par = jnp.transpose(slim[...])
     share_bias = par[0:air_h, 0:1], par[0:sea_h, 1:2]
 
-    def lay_out(first_raw, second_raw, w1, w1t, w2, w2t):
-        hidden, deep = first_raw.shape[2], w1.shape[1] // 3
+    def lay_out_first(raw_w, w1):
+        hidden, deep = raw_w.shape[2], w1.shape[1] // 3
+        blank = jnp.zeros((deep - raw_w.shape[1], hidden), F32)
+        for a in range(3):
+            tall = jnp.concatenate([raw_w[a].astype(F32), blank], axis=0)
+            w1[:, a * deep : (a + 1) * deep] = jnp.transpose(tall).astype(BF16)
+
+    def lay_out_rest(first_raw, second_raw, w1t, w2t):
+        hidden, deep = first_raw.shape[2], w2t.shape[1] // 3
         blank = jnp.zeros((deep - first_raw.shape[1], hidden), F32)
         for a in range(3):
             back = 2 - a
-            tall = lambda ref: jnp.concatenate([ref[a].astype(F32), blank], axis=0)
-            w1[:, a * deep : (a + 1) * deep] = jnp.transpose(tall(first_raw)).astype(BF16)
-            w2t[:, back * deep : (back + 1) * deep] = jnp.transpose(tall(second_raw)).astype(BF16)
+            tall = jnp.concatenate([second_raw[a].astype(F32), blank], axis=0)
+            w2t[:, back * deep : (back + 1) * deep] = jnp.transpose(tall).astype(BF16)
             w1t[:, back * hidden : (back + 1) * hidden] = first_raw[a]
+
+    def lay_out_second(second_raw, w2):
+        hidden = second_raw.shape[2]
+        for a in range(3):
             w2[:, a * hidden : (a + 1) * hidden] = second_raw[a]
+
+    def build_table():
+        index = jnp.concatenate([index_raw[:, r, :] for r in range(rows)], axis=1)
+        weight = jnp.concatenate([weight_raw[:, r, :] for r in range(rows)], axis=1).astype(F32)
+        near = jnp.sum(weight[0:4], axis=0, keepdims=True)
+        far = jnp.sum(weight[4:8], axis=0, keepdims=True)
+        slot8 = lax.broadcasted_iota(jnp.int32, weight.shape, 0)
+        total = jnp.where(is_air, near + far, jnp.where(slot8 < 4, near, far))
+        share = weight / total
+        high = lax.shift_right_logical(index, LANES.bit_length() - 1)
+        low = index & (LANES - 1)
+        place = lax.broadcasted_iota(jnp.int32, (LANES, cells), 0)
+        wrows = values.shape[0]
+        row16 = lax.broadcasted_iota(jnp.int32, (wrows, cells), 0)
+        row16 = jnp.where(is_air, row16, row16 % (wrows // 2))
+        for s in range(8):
+            onehot[:, s * cells : (s + 1) * cells] = jnp.where(
+                place == low[s : s + 1], 1.0, 0.0).astype(BF16)
+            share_hi[:, s * cells : (s + 1) * cells] = jnp.where(
+                row16 == high[s : s + 1], share[s : s + 1], 0.0)
 
     @pl.when(is_air)
     def _():
         for c in fetch[10:12]:
             c.wait()
-        lay_out(aw1_raw, aw2_raw, aw1, aw1t, aw2, aw2t)
+        lay_out_first(aw1_raw, aw1)
+        lay_out_second(aw2_raw, aw2)
 
     @pl.when(is_sea)
     def _():
         for c in fetch[12:14]:
             c.wait()
-        lay_out(sw1_raw, sw2_raw, sw1, sw1t, sw2, sw2t)
-
-    near = jnp.sum(weight[0:4], axis=0, keepdims=True)
-    far = jnp.sum(weight[4:8], axis=0, keepdims=True)
-    slot8 = lax.broadcasted_iota(jnp.int32, weight.shape, 0)
-    total = jnp.where(is_air, near + far, jnp.where(slot8 < 4, near, far))
-    share = weight / total
-    high = lax.shift_right_logical(index, LANES.bit_length() - 1)
-    low = index & (LANES - 1)
-    place = lax.broadcasted_iota(jnp.int32, (LANES, cells), 0)
+        lay_out_first(sw1_raw, sw1)
+        lay_out_second(sw2_raw, sw2)
+        lay_out_rest(sw1_raw, sw2_raw, sw1t, sw2t)
+        build_table()
+
     wrows = values.shape[0]
-    row16 = lax.broadcasted_iota(jnp.int32, (wrows, cells), 0)
-    row16 = jnp.where(is_air, row16, row16 % (wrows // 2))
-    for s in range(8):
-        onehot[:, s * cells : (s + 1) * cells] = jnp.where(
-            place == low[s : s + 1], 1.0, 0.0).astype(BF16)
-        share_hi[:, s * cells : (s + 1) * cells] = jnp.where(
-            row16 == high[s : s + 1], share[s : s + 1], 0.0)
-
     per = columns // LANES
 
     def gather():
@@ -381,23 +397,26 @@
         pay[1:2, :] = jnp.sum(flux1 * y, axis=0, keepdims=True)
         for c in pays:
             c.start()
+        build_table()
+        lay_out_rest(aw1_raw, aw2_raw, aw1t, aw2t)
         for c in pays:
             c.wait_recv()
         near, far = gather()
         lifted = jnp.sum(near + far, axis=0, keepdims=True)
         image = (y + react * lifted).astype(BF16)
         wide = image.astype(F32)
-        give(image_ref, wide)
         surface = jnp.sum(react * wide, axis=0, keepdims=True)
         source = jnp.broadcast_to(surface, (wrows, cells))
         scatter(source, source)
         for c in wins:
             c.start()
+        give(image_ref, wide)
         for c in wins:
             c.wait_recv()
         back0, back1 = arrived()
         total = wide + (flux0 * back0 + flux1 * back1)
         cot[...] = total.astype(BF16)
+        start(halo_b, TILE_WAYS)
         edge_b[...] = pack_edges(cot[...].astype(F32), rows, columns)
 
     @pl.when(is_sea)
@@ -425,9 +444,10 @@
             c.start()
         image = jnp.concatenate(images, axis=0).astype(BF16)
         cot[...] = image
+        start(halo_b, TILE_WAYS)
         edge_b[...] = pack_edges(image.astype(F32), rows, columns)
 
-    start(halo_b)
+    start(halo_b, EDGE_WAYS)
 
     @pl.when(is_sea)
     def _():

time: 36.6 us -> 36.5 us (level)
  no operation moved by 1% of the time
where the time goes in v2:
time: 36.5 us; the launch traced here: 36.3 us
  Pallas kernels  33.4 us (92%)
  local copies, waits for them, and re-layouts  2.25 us (6%)
  between operations  0.65 us (2%)
    pallas_call x1, Pallas kernels, shards(): pl.pallas_call(functools.partial(kernel, (rows, columns, lat_n, lon_n, ai...  33.4 us
    unnamed x4, local copies, waits for them, and re-layouts  2.25 us

profile of v2, /device:TPU:1, one launch (start us, length us, event | category | flops | bytes accessed | tf_op | source)
XLA Modules:
  0.0 36.3 jit_solution(6677774418879226582)
XLA Ops:
  0.6 33.4 %coupled.1 = (bf16[80,2,256]{2,1,0:T(2,128)(2,1)}, bf16[80,2,256]{2,1,0:T(2,128)(2,1)}) custom-call(bf16[80,2,256]{2,1,0:T(2,128)(2,1)} %bitcast.22, bf16[80,2,256]{2,1,0:T(2,128)(2,1)} %bitcast.23, s32[8,2,256]{2,1,0:T(2,128)} %bitcast.26, s32[8,2,256]{2,1,0:T(2,128)} %bitcast.27, s32[2,2,256]{2,1,0:T(2,128)} %mask_hbm.1, f32[1,512]{1,0:T(1,128)} %bitcast.28, ...), custom_call_target="tpu_custom_call" | custom-call | tf_op jit(solution)/shard_map/coupled/pallas_call | solution.py:505
  34.1 0.0 copy-start
  34.1 1.6 %copy.18 = bf16[1,80,2,256]{3,2,1,0:T(2,128)(2,1)} copy(bf16[1,80,2,256]{3,2,1,0:T(2,128)(2,1)} %bitcast.25) | data formatting | bytes 163840
  35.7 0.0 copy-done
  35.7 0.6 %copy.19 = bf16[1,80,2,256]{3,2,1,0:T(2,128)(2,1)} copy(bf16[1,80,2,256]{3,2,1,0:T(2,128)(2,1)S(1)} %bitcast.24) | data formatting | bytes 163840
Async XLA Ops:
  34.1 1.6 %copy-start = (bf16[80,2,256]{2,1,0:T(2,128)(2,1)S(1)}, bf16[80,2,256]{2,1,0:T(2,128)(2,1)}, u32[]{:S(2)}) copy-start(bf16[80,2,256]{2,1,0:T(2,128)(2,1)} %get-tuple-element.5) | copy-start | bytes 245764

commit v3 on v2

--- a/solution.py
+++ b/solution.py
@@ -355,27 +355,38 @@
 
     def first_conv(w1, bias, x, v, slope, z, height):
         def body(p, carry):
-            pre = dot(w1[...], rows_of(x, p)) + bias
+            both = dot(w1[...], jnp.concatenate([rows_of(x, p), rows_of(v, p)], axis=1))
+            width = x.shape[2]
+            pre, lin = both[:, :width] + bias, both[:, width:]
             t = jnp.tanh(pre)
             s = 1.0 - t * t
             slope[p] = s
-            lin = dot(w1[...], rows_of(v, p))
             z[p] = (s * keep(p, height) * lin).astype(BF16)
             return carry
         lax.fori_loop(0, height + 2, body, 0)
 
+    def two_rows(w, z, height, forward):
+        out, width = [], z.shape[2]
+        for i in range(0, height, 2):
+            both = dot(w[...], jnp.concatenate([rows_of(z, i), rows_of(z, i + 1)], axis=1))
+            out += [fold_three(both[:, :width], forward, columns),
+                    fold_three(both[:, width:], forward, columns)]
+        return out
+
     def second_conv(w2, z, height):
-        return [fold_three(dot(w2[...], rows_of(z, i)), True, columns) for i in range(height)]
+        return two_rows(w2, z, height, True)
 
     def second_back(w2t, c, slope, z, height):
-        def body(p, carry):
-            lin = dot(w2t[...], rows_of(c, p))
-            z[p] = (slope[p] * keep(p, height) * lin).astype(BF16)
+        def body(pair, carry):
+            p, width = 2 * pair, c.shape[2]
+            both = dot(w2t[...], jnp.concatenate([rows_of(c, p), rows_of(c, p + 1)], axis=1))
+            z[p] = (slope[p] * keep(p, height) * both[:, :width]).astype(BF16)
+            z[p + 1] = (slope[p + 1] * keep(p + 1, height) * both[:, width:]).astype(BF16)
             return carry
-        lax.fori_loop(0, height + 2, body, 0)
+        lax.fori_loop(0, (height + 2) // 2, body, 0)
 
     def first_back(w1t, z, height):
-        return [fold_three(dot(w1t[...], rows_of(z, i)), False, columns) for i in range(height)]
+        return two_rows(w1t, z, height, False)
 
     def packed(fine, split):
         parts = [jnp.concatenate(fine[s * rows : (s + 1) * rows], axis=1) for s in range(split)]

time: 36.5 us -> 34.7 us (0.951)
  Pallas kernels: 33.4 us -> 31.7 us
    pallas_call x1, Pallas kernels: 33.4 us -> 31.7 us  [shards(): pl.pallas_call(functools.partial(kernel, (rows, columns, lat_n, lon_n, ai...]
where the time goes in v3:
time: 34.7 us; the launch traced here: 34.6 us
  Pallas kernels  31.7 us (91%)
  local copies, waits for them, and re-layouts  2.25 us (6%)
  between operations  0.65 us (2%)
    pallas_call x1, Pallas kernels, shards(): pl.pallas_call(functools.partial(kernel, (rows, columns, lat_n, lon_n, ai...  31.7 us
    unnamed x4, local copies, waits for them, and re-layouts  2.25 us

profile of v3, /device:TPU:1, one launch (start us, length us, event | category | flops | bytes accessed | tf_op | source)
XLA Modules:
  0.0 34.6 jit_solution(16278306974814968202)
XLA Ops:
  0.6 31.7 %coupled.1 = (bf16[80,2,256]{2,1,0:T(2,128)(2,1)}, bf16[80,2,256]{2,1,0:T(2,128)(2,1)}) custom-call(bf16[80,2,256]{2,1,0:T(2,128)(2,1)} %bitcast.22, bf16[80,2,256]{2,1,0:T(2,128)(2,1)} %bitcast.23, s32[8,2,256]{2,1,0:T(2,128)} %bitcast.26, s32[8,2,256]{2,1,0:T(2,128)} %bitcast.27, s32[2,2,256]{2,1,0:T(2,128)} %mask_hbm.1, f32[1,512]{1,0:T(1,128)} %bitcast.28, ...), custom_call_target="tpu_custom_call" | custom-call | tf_op jit(solution)/shard_map/coupled/pallas_call | solution.py:516
  32.3 0.0 copy-start
  32.3 1.6 %copy.18 = bf16[1,80,2,256]{3,2,1,0:T(2,128)(2,1)} copy(bf16[1,80,2,256]{3,2,1,0:T(2,128)(2,1)} %bitcast.25) | data formatting | bytes 163840
  33.9 0.0 copy-done
  33.9 0.6 %copy.19 = bf16[1,80,2,256]{3,2,1,0:T(2,128)(2,1)} copy(bf16[1,80,2,256]{3,2,1,0:T(2,128)(2,1)S(1)} %bitcast.24) | data formatting | bytes 163840
Async XLA Ops:
  32.3 1.6 %copy-start = (bf16[80,2,256]{2,1,0:T(2,128)(2,1)S(1)}, bf16[80,2,256]{2,1,0:T(2,128)(2,1)}, u32[]{:S(2)}) copy-start(bf16[80,2,256]{2,1,0:T(2,128)(2,1)} %get-tuple-element.5) | copy-start | bytes 245764
